TPU v7x, 512 devices: a whole 4x8x8 slice. The times are simulated.
512 devices in a mesh: dp: 32 (over y, z_lo, core), pipe: 16 (over z_hi, x).
Axes of the slice: x: 4, y: 8, z: 8 (z_hi: 4, z_lo: 2; z = z_hi * 2 + z_lo), core: 2. Of those that a mesh axis runs over, the one named last changes fastest.
Arguments:
- hidden: bfloat16 [2, 128, 8192], P(None, 'pipe', 'dp'), may hold values from -180 to 180
- weight: bfloat16 [65536, 8192], P('pipe', 'dp'), may hold values from -0.25 to 0.25
- targets: int32 [2, 128], replicated, may hold values from 0 to 65535
- row_grad: float32 [2, 128], replicated, may hold values from 4 to 40
Outputs:
- grad_hidden: bfloat16 [2, 128, 8192], P(None, 'pipe', 'dp')
- grad_weight: bfloat16 [65536, 8192], P('pipe', 'dp')
- row_loss: float32 [2, 128], P(None, 'dp')
All inputs are finite; a program needn't handle non-finite values.
Results may differ from a plain program's by a relative error of at most 0.006.
Values may be sent and summed in bfloat16 or wider, within the bound.
A program may use at most 64 MiB of HBM per device.

v0:
```python
import jax
import jax.numpy as jnp
from jax import lax
from jax.sharding import PartitionSpec as P


def on_device(hidden, weight, targets, row_grad):
    n_dp = lax.axis_size("dp")
    dp_idx = lax.axis_index("dp")
    pipe_idx = lax.axis_index("pipe")
    v_dev = weight.shape[0]
    batch = targets.shape[1]
    grad_acc = jnp.zeros(weight.shape, jnp.float32)
    grads = []
    losses = []
    for micro in range(2):
        h_full = lax.all_gather(hidden[micro], "pipe", axis=0, tiled=True)
        target_row = targets[micro]
        scale_row = row_grad[micro]
        share = batch // n_dp
        first = dp_idx * share
        logits = lax.psum_scatter(
            lax.dot_general(
                h_full, weight, (((1,), (1,)), ((), ())), preferred_element_type=jnp.float32
            ),
            "dp",
            scatter_dimension=0,
            tiled=True,
        )
        tgt = lax.dynamic_slice_in_dim(target_row, first, share, 0)
        scale = lax.dynamic_slice_in_dim(scale_row, first, share, 0)
        vocab_ids = pipe_idx * v_dev + jnp.arange(v_dev, dtype=jnp.int32)
        hit = tgt[:, None] == vocab_ids[None, :]
        local_max = jnp.max(logits, axis=1)
        picked_part = jnp.sum(jnp.where(hit, logits, 0.0), axis=1)
        top = lax.pmax(local_max, "pipe")
        total, picked = lax.psum(
            (jnp.sum(jnp.exp(logits - top[:, None]), axis=1), picked_part), "pipe"
        )
        losses.append(top + jnp.log(total) - picked)
        probs = jnp.exp(logits - top[:, None]) / total[:, None]
        dlogits = (scale[:, None] * (probs - hit.astype(jnp.float32))).astype(jnp.bfloat16)
        dl_all = lax.all_gather(dlogits, "dp", axis=0, tiled=True)
        grad_acc = grad_acc + lax.dot_general(
            dl_all, h_full, (((0,), (0,)), ((), ())), preferred_element_type=jnp.float32
        )
        grad_rows_out = lax.psum_scatter(
            jnp.dot(dl_all, weight, preferred_element_type=jnp.float32),
            "pipe",
            scatter_dimension=0,
            tiled=True,
        )
        grads.append(grad_rows_out.astype(jnp.bfloat16))
    return (jnp.stack(grads), grad_acc.astype(jnp.bfloat16), jnp.stack(losses))


def solution(mesh):
    placed = (P(None, "pipe", "dp"), P("pipe", "dp"), P(), P())
    return jax.shard_map(
        on_device,
        mesh=mesh,
        in_specs=placed,
        out_specs=(P(None, "pipe", "dp"), P("pipe", "dp"), P(None, "dp")),
        check_vma=False,
    )
```

profile of v0, /device:TPU:1, one launch (start us, length us, event | category | flops | bytes accessed | tf_op | source)
XLA Modules:
  0.0 754.8 jit_solution(12027007644046594191)
XLA Ops:
  7.2 0.0 copy-start
  7.2 0.0 all-reduce.7.cloned.1.call-start
  7.2 0.8 fusion.22
  8.1 43.1 %all-gather = bf16[1,128,256]{2,1,0:T(8,128)(2,1)S(1)} all-gather(bf16[1,8,256]{2,1,0:T(8,128)(2,1)S(1)} %get-tuple-element.20), channel_id=2, replica_groups=mesh['dp'=32,'pipe'=16] {'pipe'}, dimensions={1}, use_global_device_ids=true | all-gather | bytes 69632 | tf_op jit(solution)/shard_map/all_gather | solution.py:17
  51.2 31.3 %all-gather.1 = bf16[1,128,256]{2,1,0:T(8,128)(2,1)S(1)} all-gather(bf16[1,8,256]{2,1,0:T(8,128)(2,1)S(1)} %get-tuple-element.19), channel_id=3, replica_groups=mesh['dp'=32,'pipe'=16] {'pipe'}, dimensions={1}, use_global_device_ids=true | all-gather | bytes 69632 | tf_op jit(solution)/shard_map/all_gather | solution.py:17
  82.5 0.0 copy-done
  82.5 2.1 fusion.10
  84.6 2.1 fusion.6
  86.8 0.0 copy-start.1
  86.8 0.0 copy-start.2
  86.8 0.0 all-reduce.7.cloned.1.call-update
  86.8 0.0 all-gather.7.cloned.1.call-start
  86.8 1.3 dynamic-slice.4
  88.8 0.0 copy-done.1
  88.8 0.1 fusion.19
  88.9 0.0 copy-done.2
  88.9 0.1 fusion.18
  89.0 252.7 %all-reduce.7.cloned.1.call-done = (f32[128,4096]{1,0:T(8,128)}, f32[128,4096]{1,0:T(8,128)}) async-done(((f32[128,4096]{1,0:T(8,128)}, f32[128,4096]{1,0:T(8,128)}), (f32[128,4096]{1,0:T(8,128)}, f32[128,4096]{1,0:T(8,128)})) %all-reduce.7.cloned.1.call-update) | async-done | bytes 4194320
  341.7 1.1 dynamic-slice_reduce_fusion
  342.8 36.9 %all-reduce.4 = (f32[4]{0:T(128)S(1)}, f32[4]{0:T(128)S(1)}) all-reduce(f32[4]{0:T(128)S(1)} %get-tuple-element.30, f32[4]{0:T(128)S(1)} %get-tuple-element.29), channel_id=1, replica_groups=mesh['dp'=32,'pipe'=16] {'pipe'}, use_global_device_ids=true, to_apply=%region_2.3 | all-reduce | flops 8 | bytes 64 | tf_op jit(solution)/shard_map/pmax | solution.py:36
  379.7 1.3 fusion.2
  381.0 32.4 %all-reduce.3 = (f32[4]{0:T(128)S(1)}, f32[4]{0:T(128)S(1)}, f32[4]{0:T(128)S(1)}, f32[4]{0:T(128)S(1)}) all-reduce(f32[4]{0:T(128)S(1)} %get-tuple-element.7, f32[4]{0:T(128)S(1)} %get-tuple-element.4, f32[4]{0:T(128)S(1)} %get-tuple-element.8, f32[4]{0:T(128)S(1)} %get-tuple-element.3), channel_id=1, replica_groups=mesh['dp'=32,'pipe'=16] {'pipe'}, use_global_device_ids=true, to_apply=%region_10.11 | all-reduce | flops 16 | bytes 128 | tf_op jit(solution)/shard_map/psum | solution.py:37
  413.4 1.7 fusion.16
  415.2 0.0 all-gather.7.cloned.1.call-update
  415.2 0.0 all-gather.9.cloned.1.call-start
  415.3 0.7 all-gather.9.cloned.1.call-update
  415.9 0.0 reduce-scatter.5.cloned.1.call-start
  416.0 0.6 pad_maximum_fusion.1
  416.6 75.9 %all-gather.7.cloned.1.call-done = bf16[32,4,4096]{2,1,0:T(4,128)(2,1)} async-done(((bf16[1,4,4096]{2,1,0:T(4,128)(2,1)}), bf16[32,4,4096]{2,1,0:T(4,128)(2,1)}) %all-gather.7.cloned.1.call-update) | async-done | bytes 1048592 | tf_op jit(solution)/shard_map/all_gather | solution.py:43
  492.5 1.3 reshape.29
  493.8 2.7 fusion.8
  496.5 64.2 %all-gather.9.cloned.1.call-done = bf16[32,4,4096]{2,1,0:T(4,128)(2,1)} async-done(((bf16[1,4,4096]{2,1,0:T(4,128)(2,1)}), bf16[32,4,4096]{2,1,0:T(4,128)(2,1)}) %all-gather.9.cloned.1.call-update) | async-done | bytes 1048592 | tf_op jit(solution)/shard_map/all_gather | solution.py:43
  560.7 2.1 reshape.31
  562.9 2.3 fusion.26
  565.2 0.0 reduce-scatter.5.cloned.1.call-update
  565.2 0.0 reduce-scatter.3.cloned.1.call-start
  565.2 1.1 fusion.25
  566.3 0.0 reduce-scatter.3.cloned.1.call-update
  566.4 4.6 fusion
  570.9 83.0 %reduce-scatter.5.cloned.1.call-done = f32[8,256]{1,0:T(8,128)} async-done(((f32[128,256]{1,0:T(8,128)}), f32[8,256]{1,0:T(8,128)}) %reduce-scatter.5.cloned.1.call-update) | async-done | bytes 8208 | tf_op jit(solution)/shard_map/reduce_scatter | solution.py:47
  654.0 0.7 convert_bitcast_fusion
  654.7 92.3 %reduce-scatter.3.cloned.1.call-done = f32[8,256]{1,0:T(8,128)} async-done(((f32[128,256]{1,0:T(8,128)}), f32[8,256]{1,0:T(8,128)}) %reduce-scatter.3.cloned.1.call-update) | async-done | bytes 8208 | tf_op jit(solution)/shard_map/reduce_scatter | solution.py:47
  747.0 0.7 convert_bitcast_fusion.1
  747.7 0.6 pad_maximum_fusion
  (5 shorter events, 0.0 us)
Async XLA Ops:
  7.2 75.3 %copy-start = (bf16[4096,256]{1,0:T(8,128)(2,1)S(1)}, bf16[4096,256]{1,0:T(8,128)(2,1)}, u32[]{:S(2)}) copy-start(bf16[4096,256]{1,0:T(8,128)(2,1)} %param.5) | copy-start | bytes 6291460
  7.2 334.5 %all-reduce.7.cloned.1.call-start = ((), (), s32[]{:S(2)}) async-start(), calls=%async_computation.6 | async-start | bytes 8388608
  86.8 2.0 copy-start.1
  86.8 2.1 copy-start.2
  86.8 405.7 %all-gather.7.cloned.1.call-start = ((), (), s32[]{:S(2)}) async-start(), calls=%async_computation.4 | async-start | bytes 1081344 | tf_op jit(solution)/shard_map/all_gather | solution.py:43
  415.2 145.5 %all-gather.9.cloned.1.call-start = ((), (), s32[]{:S(2)}) async-start(), calls=%async_computation.5 | async-start | bytes 1081344 | tf_op jit(solution)/shard_map/all_gather | solution.py:43
  415.9 238.0 %reduce-scatter.5.cloned.1.call-start = ((), (), s32[]{:S(2)}) async-start(), calls=%async_computation.3 | async-start | bytes 139264 | tf_op jit(solution)/shard_map/reduce_scatter | solution.py:47
  565.2 181.8 %reduce-scatter.3.cloned.1.call-start = ((), (), s32[]{:S(2)}) async-start(), calls=%async_computation.2 | async-start | bytes 139264 | tf_op jit(solution)/shard_map/reduce_scatter | solution.py:47
Sparse Core Ops, SparseCore 0:
  86.9 254.7 all-reduce.6
  415.3 77.0 all-gather.6
  494.6 66.0 all-gather.8
  565.3 88.6 reduce-scatter.4
  658.4 88.5 reduce-scatter.2
where the time goes:
time: 756 us; the launch traced here: 755 us
  waiting for transfers between devices  569 us (75%)
  blocking collectives  144 us (19%)
  matrix products  14.9 us (2%)
  between operations  14.5 us (2%)
    unnamed x6, waiting for transfers between devices  253 us
    reduce_scatter x2, waiting for transfers between devices, on_device(): lax.psum_scatter(jnp.dot(dl_all, weight, preferred_element_type=jnp.float...  175 us
    all_gather x2, waiting for transfers between devices, on_device(): dl_all = lax.all_gather(dlogits, 'dp', axis=0, tiled=True)  140 us
    all_gather x2, blocking collectives, on_device(): h_full = lax.all_gather(hidden[micro], 'pipe', axis=0, tiled=True)  74.4 us
    pmax x1, blocking collectives, on_device(): top = lax.pmax(local_max, 'pipe')  36.9 us
    psum x1, blocking collectives, on_device(): lax.psum((jnp.sum(jnp.exp(logits - top[:, None]), axis=1), picked_part),...  32.4 us
  transfers between devices with their start and end apart: 5, of which 5 were waited for; matrix products, arithmetic and copies ran while one was open for 2% of the time, Pallas kernels for 0%

commit v1 on v0

v1 whole, which is shorter than its diff:
```python
import functools
import math

import jax
import jax.numpy as jnp
from jax import lax
from jax.experimental import pallas as pl
from jax.experimental.pallas import tpu as pltpu
from jax.sharding import PartitionSpec as P

MESH = pl.DeviceIdType.MESH
F32, BF16, I16, I32 = jnp.float32, jnp.bfloat16, jnp.int16, jnp.int32

Y, NB, ROWS = 8, 16, 16
HALF = 2048
SUB, NSUB = 1024, 2
CODE = 128
STEP = math.log(2.0) / 256
TOP = 32766.0
CHUNK = 256


def coords():
    dp, pipe = lax.axis_index("dp"), lax.axis_index("pipe")
    return dp // 4, (dp // 2) % 2, dp % 2, pipe


def lanes_mul(x, s):
    n = x.shape[1] // 128
    return jnp.concatenate([x[:, i * 128 : (i + 1) * 128] * s for i in range(n)], axis=1)


def encode(ref, slot, x, bound):
    code = jnp.ceil(jnp.log(jnp.maximum(bound, 1e-30)) * (1.0 / STEP)) + 1.0
    inv = TOP * jnp.exp(code * -STEP)
    ref[slot, :, :SUB] = jnp.round(lanes_mul(x, inv)).astype(I32).astype(I16)
    ref[slot, :, SUB:] = code.astype(I32).astype(I16)


def decode(ref, slot):
    scale = jnp.exp(ref[slot, :, SUB:].astype(I32).astype(F32) * STEP)
    x = ref[slot, :, :SUB].astype(I32).astype(F32)
    return lanes_mul(x, scale * (1.0 / TOP)), scale


def diagonal():
    return lax.broadcasted_iota(I32, (ROWS, 128), 0) == lax.broadcasted_iota(I32, (ROWS, 128), 1)


def to_lanes(col):
    return jnp.sum(jnp.where(diagonal(), col, 0.0), axis=0, keepdims=True)


def to_rows(row):
    shape = row.shape[:-2] + (ROWS, 128)
    at = len(shape) - 2
    eye = lax.broadcasted_iota(I32, shape, at) == lax.broadcasted_iota(I32, shape, at + 1)
    return jnp.broadcast_to(
        jnp.sum(jnp.where(eye, jnp.broadcast_to(row, shape), 0.0), axis=-1, keepdims=True), shape
    )


def kernel(
    h_ref, w_ref, t_ref, g_ref, dh_ref, dw_ref, loss_ref,
    hm, hs, wm, ws, part, scale, tcol, gcol, logit, e_all, dl, dwv, acc, fcol,
    zs, zr, ls, lr, ss, sr, st0, st1, st2, mine, dhs, dhr,
    w_sem, ws_sem, hl_sem, h_send, h_recv, hf_send, hf_recv, z_send, z_recv, l_send, l_recv, s_send, s_recv,
    st_send, st_recv, az_send, az_recv, al_send, al_recv, as_send, as_recv, ac_send, ac_recv,
    d_send, d_recv, dw_sem,
):
    y, zl, c, pipe = coords()
    zh, px = pipe // 4, pipe % 4
    me_dp = y * 4 + zl * 2 + c

    def at_dp(yy, zz, cc):
        return (yy * 4 + zz * 2 + cc, pipe)

    def yo(o):
        return lax.rem(y + o + Y, Y)

    def pipe_peer(i):
        return lax.rem(zh + i // 4, 4) * 4 + lax.rem(px + i % 4, 4)

    def dp_peer(i):
        return lax.rem(y + i // 2, Y), lax.rem(zl + i % 2, 2)

    sib = at_dp(y, zl, 1 - c)
    zdev = at_dp(y, 1 - zl, c)

    def send(src, dst, s_sem, r_sem, dev):
        cp = pltpu.make_async_remote_copy(
            src_ref=src, dst_ref=dst, send_sem=s_sem, recv_sem=r_sem, device_id=dev, device_id_type=MESH
        )
        cp.start()
        return cp

    w_copy = pltpu.make_async_copy(w_ref, wm, w_sem)
    w_copy.start()
    h_copy = pltpu.make_async_copy(h_ref, hm.at[pipe], hl_sem)
    h_copy.start()

    barrier = pltpu.get_barrier_semaphore()

    @pl.loop(1, 16)
    def _(i):
        pl.semaphore_signal(barrier, inc=1, device_id=(me_dp, pipe_peer(i)), device_id_type=MESH)
        yy, zz = dp_peer(i)
        pl.semaphore_signal(barrier, inc=1, device_id=at_dp(yy, zz, c), device_id_type=MESH)

    pl.semaphore_signal(barrier, inc=1, device_id=sib, device_id_type=MESH)

    shape = (NB, ROWS, 128)
    b_id, r_id = lax.broadcasted_iota(I32, shape, 0), lax.broadcasted_iota(I32, shape, 1)
    lane = lax.broadcasted_iota(I32, shape, 2)
    pick = lane == b_id * 8 + r_id % 8
    first = r_id < 8

    def column(ref):
        x = ref[...].astype(F32)
        x = jnp.where(first, x[0:1].reshape(1, 1, 128), x[1:2].reshape(1, 1, 128))
        return jnp.broadcast_to(jnp.sum(jnp.where(pick, x, 0.0), axis=-1, keepdims=True), shape)

    tcol[...] = column(t_ref).astype(I32)
    gcol[...] = column(g_ref)

    pl.semaphore_wait(barrier, 31)

    h_copy.wait()

    @pl.loop(1, 16)
    def _(i):
        send(hm.at[pipe], hm.at[pipe], h_send, h_recv.at[i // 4], (me_dp, pipe_peer(i)))

    half_rows = pl.ds(pl.multiple_of((1 - c) * HALF, HALF), HALF)
    w_swap = send(w_ref.at[half_rows], ws, ws_sem.at[0], ws_sem.at[1], sib)

    forwards = []
    for n, dz in enumerate((0, 1, 3, 2)):
        group = pl.ds(lax.rem(zh + 4 - dz, 4) * 4, 4)
        count = 3 if dz == 0 else 4
        some = hm.at[pl.ds(0, count)]
        pltpu.make_async_copy(some, some, h_recv.at[dz]).wait()
        forwards.append(send(hm.at[group], hs.at[group], hf_send.at[n], hf_recv.at[n], sib))
    for n, dz in enumerate((0, 1, 3, 2)):
        group = pl.ds(lax.rem(zh + 4 - dz, 4) * 4, 4)
        forwards[n].wait_recv()
    w_copy.wait()
    w_swap.wait_recv()

    scale[...] = jnp.zeros(shape, F32)
    hm_all = hm[...].reshape(NB * ROWS, CHUNK)
    hs_all = hs[...].reshape(NB * ROWS, CHUNK)
    nt = (((1,), (1,)), ((), ()))

    @pl.loop(0, HALF // CHUNK)
    def _(k):
        own = pl.ds(pl.multiple_of(c * HALF + k * CHUNK, CHUNK), CHUNK)
        there = pl.ds(pl.multiple_of(k * CHUNK, CHUNK), CHUNK)
        x = lax.dot_general(hm[...].reshape(NB * ROWS, CHUNK), wm[own, :], nt, preferred_element_type=F32)
        x += lax.dot_general(hs[...].reshape(NB * ROWS, CHUNK), ws[there, :], nt, preferred_element_type=F32)
        x = x.reshape(NB, ROWS, CHUNK)
        part[:, :, there] = x
        scale[...] = jnp.maximum(scale[...], jnp.maximum(jnp.abs(x[..., :128]), jnp.abs(x[..., 128:])))

    scale[...] = jnp.broadcast_to(jnp.max(scale[...], axis=-1, keepdims=True), shape)

    signs = (1, -1)
    order = (4, 3, -3, 2, -2, 1, -1, 0)
    pending = []

    def block(o, zz):
        return yo(o) * 2 + zz

    def own_part(b, u):
        return part[b, :, u * SUB : (u + 1) * SUB]

    zsend, zrecv = {}, {}
    for n, o in enumerate(order):
        for u in range(NSUB):
            b = block(o * signs[u], 1 - zl)
            slot = n * NSUB + u
            encode(zs, slot, own_part(b, u), scale[b])
            zrecv[o, u] = send(zs.at[slot], zr.at[slot], z_send.at[slot], z_recv.at[slot], zdev)
            pending.append(zrecv[o, u])

    def with_z(o, u):
        b = block(o * signs[u], zl)
        slot = order.index(o) * NSUB + u
        zrecv[o, u].wait_recv()
        x, s = decode(zr, slot)
        return own_part(b, u) + x, scale[b] + s

    long, short = {}, {}
    for k in range(1, 5):
        for u in range(NSUB):
            x, s = with_z(5 - k, u)
            slot = (k - 1) * NSUB + u
            if k > 1:
                long[k - 1, u].wait_recv()
                more, more_s = decode(lr, slot - NSUB)
                x, s = x + more, s + more_s
            encode(ls, slot, x, s)
            long[k, u] = send(
                ls.at[slot], lr.at[slot], l_send.at[slot], l_recv.at[slot], at_dp(yo(signs[u]), zl, c)
            )
            pending.append(long[k, u])
        if k > 3:
            continue
        for u in range(NSUB):
            x, s = with_z(k - 4, u)
            slot = (k - 1) * NSUB + u
            if k > 1:
                short[k - 1, u].wait_recv()
                more, more_s = decode(sr, slot - NSUB)
                x, s = x + more, s + more_s
            encode(ss, slot, x, s)
            short[k, u] = send(
                ss.at[slot], sr.at[slot], s_send.at[slot], s_recv.at[slot], at_dp(yo(-signs[u]), zl, c)
            )
            pending.append(short[k, u])
    for u in range(NSUB):
        x, _ = with_z(0, u)
        short[3, u].wait_recv()
        x += decode(sr, 2 * NSUB + u)[0]
        long[4, u].wait_recv()
        x += decode(lr, 3 * NSUB + u)[0]
        logit[:, u * SUB : (u + 1) * SUB] = x

    mb = y * 2 + zl
    x = logit[...]
    m_col = jnp.max(x, axis=1, keepdims=True)
    e = jnp.exp(x - m_col)
    s_col = jnp.sum(e, axis=1, keepdims=True)
    ids = pipe * (2 * HALF) + c * HALF + lax.broadcasted_iota(I32, x.shape, 1)
    hit = ids == jnp.concatenate([tcol[mb]] * (HALF // 128), axis=1)
    p_col = jnp.sum(jnp.where(hit, x, 0.0), axis=1, keepdims=True)
    for u in range(NSUB):
        e_all[c, u, mb] = e[:, u * SUB : (u + 1) * SUB].astype(BF16)

    wide = (ROWS, 128)
    stats = [to_lanes(jnp.broadcast_to(v, wide)) for v in (m_col, s_col, p_col)]

    glong, gshort, gz = {}, {}, {}

    def chunk(u, b):
        return e_all.at[c, u, b]

    def to_core(u, b, n):
        cp = send(chunk(u, b), chunk(u, b), ac_send, ac_recv, sib)
        return cp

    def to_z(u, o):
        b = block(o * signs[u], zl)
        slot = order.index(o) * NSUB + u
        gz[o, u] = send(chunk(u, b), chunk(u, b), az_send.at[slot], az_recv.at[slot], zdev)
        pending.append(gz[o, u])

    def from_z(u, o):
        b = block(o * signs[u], 1 - zl)
        slot = order.index(o) * NSUB + u
        pltpu.make_async_copy(chunk(u, b), chunk(u, b), az_recv.at[slot]).wait()
        to_core(u, b, slot)

    def go_long(u, k):
        b = block(-(k - 1) * signs[u], zl)
        slot = (k - 1) * NSUB + u
        glong[k, u] = send(chunk(u, b), chunk(u, b), al_send.at[slot], al_recv.at[slot], at_dp(yo(signs[u]), zl, c))
        pending.append(glong[k, u])

    def go_short(u, k):
        b = block((k - 1) * signs[u], zl)
        slot = (k - 1) * NSUB + u
        gshort[k, u] = send(chunk(u, b), chunk(u, b), as_send.at[slot], as_recv.at[slot], at_dp(yo(-signs[u]), zl, c))
        pending.append(gshort[k, u])

    def got(sem, slot, u, b):
        pltpu.make_async_copy(chunk(u, b), chunk(u, b), sem.at[slot]).wait()

    def step(k):
        for u in range(NSUB):
            b = block(-k * signs[u], zl)
            got(al_recv, (k - 1) * NSUB + u, u, b)
            if k < 4:
                go_long(u, k + 1)
            to_z(u, -k if k < 4 else 4)
            to_core(u, b, None)
        if k < 4:
            for u in range(NSUB):
                b = block(k * signs[u], zl)
                got(as_recv, (k - 1) * NSUB + u, u, b)
                if k < 3:
                    go_short(u, k + 1)
                to_z(u, k)
                to_core(u, b, None)

    for u in range(NSUB):
        go_long(u, 1)
        go_short(u, 1)
        to_z(u, 0)
        to_core(u, mb, None)

    for n in range(3):
        mine[0, :, n * 128 : (n + 1) * 128] = stats[n]
    both = send(mine.at[0], st0.at[0], st_send.at[0], st_recv.at[0], sib)
    pending.append(both)
    both.wait_recv()
    other = [st0[0, :, n * 128 : (n + 1) * 128] for n in range(3)]
    m_two = jnp.maximum(stats[0], other[0])
    s_two = stats[1] * jnp.exp(stats[0] - m_two) + other[1] * jnp.exp(other[0] - m_two)
    p_two = stats[2] + other[2]
    for n, v in enumerate((m_two, s_two, p_two)):
        st1[pipe, :, n * 128 : (n + 1) * 128] = v

    @pl.loop(1, 16)
    def _(i):
        send(st1.at[pipe], st1.at[pipe], st_send.at[1], st_recv.at[1], (me_dp, pipe_peer(i)))

    step(1)
    for u in range(NSUB):
        from_z(u, 0)
    step(2)

    fifteen = st1.at[pl.ds(0, 15)]
    pltpu.make_async_copy(fifteen, fifteen, st_recv.at[1]).wait()
    ms, sums, picks = (st1[:, 0, n * 128 : (n + 1) * 128] for n in range(3))
    top = jnp.max(ms, axis=0, keepdims=True)
    total = jnp.sum(sums * jnp.exp(ms - top), axis=0, keepdims=True)
    picked = jnp.sum(picks, axis=0, keepdims=True)
    live = lax.broadcasted_iota(I32, (1, 128), 1) < ROWS
    total = jnp.where(live, total, 1.0)
    g = to_lanes(gcol[mb])
    f_mine = g * (jnp.exp(stats[0] - top) / total)
    f_other = g * (jnp.exp(other[0] - top) / total)
    at_hit = g * (jnp.exp(picked - top) / total - 1.0)
    loss = top + jnp.log(total) - picked
    is0 = c == 0
    st2[mb, :, 0:128] = jnp.where(is0, f_mine, f_other)
    st2[mb, :, 128:256] = jnp.where(is0, f_other, f_mine)
    st2[mb, :, 256:384] = at_hit

    @pl.loop(1, 16)
    def _(i):
        yy, zz = dp_peer(i)
        send(st2.at[mb], st2.at[mb], st_send.at[2], st_recv.at[2], at_dp(yy, zz, c))

    loss_col = to_rows(loss)
    r2, l2 = lax.broadcasted_iota(I32, wide, 0), lax.broadcasted_iota(I32, wide, 1)
    loss_out = jnp.where(r2 % 8 == 4 * c + l2, loss_col, 0.0).reshape(2, 8, 128)
    loss_ref[...] = jnp.sum(loss_out, axis=1)[:, 0:4]

    for u in range(NSUB):
        from_z(u, -1)
        from_z(u, 1)
    step(3)
    for u in range(NSUB):
        from_z(u, -2)
        from_z(u, 2)
    step(4)
    for u in range(NSUB):
        from_z(u, -3)
        from_z(u, 3)

    fifteen2 = st2.at[pl.ds(0, 15)]
    pltpu.make_async_copy(fifteen2, fifteen2, st_recv.at[2]).wait()
    for n in range(3):
        fcol[n] = to_rows(st2[:, :, n * 128 : (n + 1) * 128])
    for u in range(NSUB):
        from_z(u, 4)
    there = e_all.at[1 - c]
    pltpu.make_async_copy(there, there, ac_recv).wait()

    acc[...] = jnp.zeros(acc.shape, F32)
    full = (NB * ROWS, CHUNK)

    def twice(x):
        x = x.reshape(NB * ROWS, 128)
        return jnp.concatenate([x, x], axis=1)

    @pl.loop(0, 2 * HALF // CHUNK)
    def _(q):
        hh, u, k = q // 8, (q // 4) % 2, q % 4
        lanes = pl.ds(pl.multiple_of(k * CHUNK, CHUNK), CHUNK)
        e = e_all[hh, u, :, :, lanes].reshape(full).astype(F32)
        ids = pipe * (2 * HALF) + q * CHUNK + lax.broadcasted_iota(I32, full, 1)
        d = jnp.where(ids == twice(tcol[...]), twice(fcol[2]), e * twice(fcol[hh])).astype(BF16)
        cols = pl.ds(pl.multiple_of(q * CHUNK, CHUNK), CHUNK)
        dl[:, cols] = d
        acc[...] += jnp.dot(d, wm[cols, :], preferred_element_type=F32)

    bound = 0.51 * jnp.abs(fcol[2]) + 1e-6 * gcol[...]
    q16 = lanes_mul(acc[...], (TOP / bound).reshape(NB * ROWS, 128))
    q16 = jnp.round(jnp.clip(q16, -TOP, TOP)).astype(I32).astype(I16)
    dhs[...] = q16.reshape(NB, ROWS, CHUNK)

    @pl.loop(1, 16)
    def _(i):
        to = pipe_peer(i)
        send(dhs.at[to], dhr.at[pipe], d_send, d_recv, (me_dp, to))

    tn = (((0,), (0,)), ((), ()))

    @pl.loop(0, 2 * HALF // CHUNK)
    def _(q):
        cols = pl.ds(pl.multiple_of(q * CHUNK, CHUNK), CHUNK)
        x = lax.dot_general(dl[:, cols], hm[...].reshape(full), tn, preferred_element_type=F32)
        dwv[cols, :] = x.astype(BF16)
        pltpu.make_async_copy(dwv.at[cols], dw_ref.at[cols], dw_sem).start()

    dhr[pipe] = dhs[pipe]
    got15 = dhr.at[pl.ds(0, 15)]
    pltpu.make_async_copy(got15, got15, d_recv).wait()
    dh = jnp.sum(dhr[...].astype(I32).astype(F32), axis=0)
    own_bound = 0.51 * jnp.abs(fcol[2, pipe]) + 1e-6 * gcol[pipe]
    dh_ref[...] = lanes_mul(dh, own_bound * (1.0 / TOP)).astype(BF16)

    pltpu.make_async_copy(dwv, dw_ref, dw_sem).wait()
    for cp in pending:
        cp.wait_send()
    for cp in forwards:
        cp.wait_send()
    w_swap.wait_send()
    some = hm.at[pl.ds(0, 15)]
    pltpu.make_async_copy(some, some, h_send).wait()
    pltpu.make_async_copy(fifteen, fifteen, st_send.at[1]).wait()
    pltpu.make_async_copy(fifteen2, fifteen2, st_send.at[2]).wait()
    whole = e_all.at[c]
    pltpu.make_async_copy(whole, whole, ac_send).wait()
    pltpu.make_async_copy(got15, got15, d_send).wait()


def call(hidden, weight, targets, row_grad):
    dma = pltpu.SemaphoreType.DMA
    msg = (ROWS, SUB + CODE)
    vmem = pl.BlockSpec(memory_space=pltpu.VMEM)
    hbm = pl.BlockSpec(memory_space=pl.ANY)
    return pl.pallas_call(
        kernel,
        out_shape=(
            jax.ShapeDtypeStruct((ROWS, CHUNK), BF16),
            jax.ShapeDtypeStruct((2 * HALF, CHUNK), BF16),
            jax.ShapeDtypeStruct((2, 4), F32),
        ),
        in_specs=[vmem, hbm, vmem, vmem],
        out_specs=(vmem, hbm, vmem),
        scratch_shapes=[
            pltpu.VMEM((NB, ROWS, CHUNK), BF16),
            pltpu.VMEM((NB, ROWS, CHUNK), BF16),
            pltpu.VMEM((2 * HALF, CHUNK), BF16),
            pltpu.VMEM((HALF, CHUNK), BF16),
            pltpu.VMEM((NB, ROWS, HALF), F32),
            pltpu.VMEM((NB, ROWS, 128), F32),
            pltpu.VMEM((NB, ROWS, 128), I32),
            pltpu.VMEM((NB, ROWS, 128), F32),
            pltpu.VMEM((ROWS, HALF), F32),
            pltpu.VMEM((2, NSUB, NB, ROWS, SUB), BF16),
            pltpu.VMEM((NB * ROWS, 2 * HALF), BF16),
            pltpu.VMEM((2 * HALF, CHUNK), BF16),
            pltpu.VMEM((NB * ROWS, CHUNK), F32),
            pltpu.VMEM((3, NB, ROWS, 128), F32),
            pltpu.VMEM((8 * NSUB,) + msg, I16),
            pltpu.VMEM((8 * NSUB,) + msg, I16),
            pltpu.VMEM((4 * NSUB,) + msg, I16),
            pltpu.VMEM((4 * NSUB,) + msg, I16),
            pltpu.VMEM((3 * NSUB,) + msg, I16),
            pltpu.VMEM((3 * NSUB,) + msg, I16),
            pltpu.VMEM((1, 1, 384), F32),
            pltpu.VMEM((NB, 1, 384), F32),
            pltpu.VMEM((NB, 1, 384), F32),
            pltpu.VMEM((1, 1, 384), F32),
            pltpu.VMEM((NB, ROWS, CHUNK), I16),
            pltpu.VMEM((NB, ROWS, CHUNK), I16),
            dma, dma((2,)), dma, dma, dma((4,)), dma((4,)), dma((4,)),
            dma((8 * NSUB,)), dma((8 * NSUB,)), dma((4 * NSUB,)), dma((4 * NSUB,)), dma((3 * NSUB,)), dma((3 * NSUB,)),
            dma((3,)), dma((3,)),
            dma((8 * NSUB,)), dma((8 * NSUB,)), dma((4 * NSUB,)), dma((4 * NSUB,)), dma((3 * NSUB,)), dma((3 * NSUB,)),
            dma, dma, dma, dma, dma,
        ],
        compiler_params=pltpu.CompilerParams(
            collective_id=0, has_side_effects=True, vmem_limit_bytes=48 << 20
        ),
        cost_estimate=pl.CostEstimate(flops=1_600_000_000, bytes_accessed=5 << 20, transcendentals=1 << 20),
        name="output_layer",
    )(hidden, weight, targets, row_grad)


def on_device(hidden, weight, targets, row_grad):
    grad_hidden, grad_weight, row_loss = call(hidden.reshape(ROWS, CHUNK), weight, targets, row_grad)
    return grad_hidden.reshape(2, 8, CHUNK), grad_weight, row_loss


def solution(mesh):
    placed = (P(None, "pipe", "dp"), P("pipe", "dp"), P(), P())
    return jax.shard_map(
        on_device,
        mesh=mesh,
        in_specs=placed,
        out_specs=(P(None, "pipe", "dp"), P("pipe", "dp"), P(None, "dp")),
        check_vma=False,
    )
```

time: 756 us -> 78.9 us (0.10)
  waiting for transfers between devices: 569 us -> 0 us
  blocking collectives: 144 us -> 0 us
  Pallas kernels: 0 us -> 71.9 us
  matrix products: 14.9 us -> 0 us
  between operations: 14.5 us -> 0.65 us
    unnamed x6 -> x0, waiting for transfers between devices: 253 us -> none
    reduce_scatter x2 -> x0, waiting for transfers between devices: 175 us -> none  [on_device(): lax.psum_scatter(jnp.dot(dl_all, weight, preferred_element_type=jnp.float...]
    all_gather x2 -> x0, waiting for transfers between devices: 140 us -> none  [on_device(): dl_all = lax.all_gather(dlogits, 'dp', axis=0, tiled=True)]
    all_gather x2 -> x0, blocking collectives: 74.4 us -> none  [on_device(): h_full = lax.all_gather(hidden[micro], 'pipe', axis=0, tiled=True)]
    pallas_call x0 -> x1, Pallas kernels: none -> 71.9 us  [call(): pl.pallas_call(kernel, out_shape=(jax.ShapeDtypeStruct((ROWS, CHUNK), BF1...]
    pmax x1 -> x0, blocking collectives: 36.9 us -> none  [on_device(): top = lax.pmax(local_max, 'pipe')]
    psum x1 -> x0, blocking collectives: 32.4 us -> none  [on_device(): lax.psum((jnp.sum(jnp.exp(logits - top[:, None]), axis=1), picked_part),...]
    dot_general x6 -> x0, matrix products: 14.9 us -> none  [the longest x2 7.23 us: on_device(): lax.dot_general(dl_all, h_full, (((0,), (0,)), ((), ())), preferred_eleme...]
  transfers between devices with their start and end apart: 5 -> 0, of which waited for: 5 -> 0; matrix products, arithmetic and copies ran while one was open for 2% -> 0% of each run, Pallas kernels for 0% -> 0%
where the time goes in v1:
time: 78.9 us; the launch traced here: 78.6 us
  Pallas kernels  71.9 us (91%)
  local copies, waits for them, and re-layouts  6.12 us (8%)
    pallas_call x1, Pallas kernels, call(): pl.pallas_call(kernel, out_shape=(jax.ShapeDtypeStruct((ROWS, CHUNK), BF1...  71.9 us
    unnamed x11, local copies, waits for them, and re-layouts  6.12 us

profile of v1, /device:TPU:1, one launch (start us, length us, event | category | flops | bytes accessed | tf_op | source)
XLA Modules:
  0.0 78.6 jit_solution(16151926162774391835)
XLA Ops:
  0.6 0.0 copy-start
  0.6 1.6 %copy-done = bf16[4096,256]{1,0:T(8,128)(2,1)S(1)} copy-done((bf16[4096,256]{1,0:T(8,128)(2,1)S(1)}, bf16[4096,256]{1,0:T(8,128)(2,1)}, u32[]{:S(2)}) %copy-start) | copy-done | bytes 2097176
  2.2 0.0 copy-start.1
  2.2 0.7 copy-done.1
  2.9 0.0 copy-start.2
  2.9 0.7 copy-done.2
  3.6 0.0 copy-start.3
  3.6 0.7 copy-done.3
  4.3 71.9 %output_layer.1 = (bf16[16,256]{1,0:T(8,128)(2,1)S(1)}, bf16[4096,256]{1,0:T(8,128)(2,1)S(1)}, f32[2,4]{1,0:T(2,128)S(1)}) custom-call(bf16[16,256]{1,0:T(8,128)(2,1)S(1)} %bitcast.3, bf16[4096,256]{1,0:T(8,128)(2,1)S(1)} %copy-done, s32[2,128]{1,0:T(2,128)S(1)} %copy-done.2, f32[2,128]{1,0:T(2,128)S(1)} %copy-done.3), custom_call_target="tpu_custom_call" | custom-call | flops 1600000000 | bytes 5242880 | tf_op jit(solution)/shard_map/output_layer/pallas_call | solution.py:436
  76.2 0.6 copy.10
  76.8 1.3 %copy.11 = bf16[4096,256]{1,0:T(8,128)(2,1)} copy(bf16[4096,256]{1,0:T(8,128)(2,1)S(1)} %get-tuple-element.13) | data formatting | bytes 4194304
  78.1 0.6 copy.12
Async XLA Ops:
  0.6 1.6 %copy-start = (bf16[4096,256]{1,0:T(8,128)(2,1)S(1)}, bf16[4096,256]{1,0:T(8,128)(2,1)}, u32[]{:S(2)}) copy-start(bf16[4096,256]{1,0:T(8,128)(2,1)} %w_ref.1) | copy-start | bytes 6291460
  2.2 0.7 copy-start.1
  2.9 0.7 copy-start.2
  3.6 0.7 copy-start.3

commit v2 on v0

v2 whole, which is shorter than its diff:
```python
import functools
import math

import jax
import jax.numpy as jnp
from jax import lax
from jax.experimental import pallas as pl
from jax.experimental.pallas import tpu as pltpu
from jax.sharding import PartitionSpec as P

MESH = pl.DeviceIdType.MESH
F32, BF16, I16, I32 = jnp.float32, jnp.bfloat16, jnp.int16, jnp.int32

Y, NB, ROWS = 8, 16, 16
HALF = 2048
SUB, NSUB = 1024, 2
CODE = 128
STEP = math.log(2.0) / 256
TOP = 32766.0
CHUNK = 256


def coords():
    dp, pipe = lax.axis_index("dp"), lax.axis_index("pipe")
    return dp // 4, (dp // 2) % 2, dp % 2, pipe


def lanes_mul(x, s):
    n = x.shape[1] // 128
    return jnp.concatenate([x[:, i * 128 : (i + 1) * 128] * s for i in range(n)], axis=1)


def encode(ref, slot, x, bound):
    code = jnp.ceil(jnp.log(jnp.maximum(bound, 1e-30)) * (1.0 / STEP)) + 1.0
    inv = TOP * jnp.exp(code * -STEP)
    ref[slot, :, :SUB] = jnp.round(lanes_mul(x, inv)).astype(I32).astype(I16)
    ref[slot, :, SUB:] = code.astype(I32).astype(I16)


def decode(ref, slot):
    scale = jnp.exp(ref[slot, :, SUB:].astype(I32).astype(F32) * STEP)
    x = ref[slot, :, :SUB].astype(I32).astype(F32)
    return lanes_mul(x, scale * (1.0 / TOP)), scale


def diagonal():
    return lax.broadcasted_iota(I32, (ROWS, 128), 0) == lax.broadcasted_iota(I32, (ROWS, 128), 1)


def to_lanes(col):
    return jnp.sum(jnp.where(diagonal(), col, 0.0), axis=0, keepdims=True)


def to_rows(row):
    shape = row.shape[:-2] + (ROWS, 128)
    at = len(shape) - 2
    eye = lax.broadcasted_iota(I32, shape, at) == lax.broadcasted_iota(I32, shape, at + 1)
    return jnp.broadcast_to(
        jnp.sum(jnp.where(eye, jnp.broadcast_to(row, shape), 0.0), axis=-1, keepdims=True), shape
    )


WAYS = ((4, 2), (3, 1), (-3, -1), (1, 1), (-1, -1), (2, 2), (-2, -2))
ORDER = (4, 3, -3, 2, -2, 1, -1, 0)
SIGNS = (1, -1)


def kernel(h_ref, w_ref, t_ref, g_ref, dh_ref, dw_ref, loss_ref, v, s):
    y, zl, c, pipe = coords()
    zh, px = pipe // 4, pipe % 4
    me_dp = y * 4 + zl * 2 + c
    mb = y * 2 + zl
    hm, hs, wm, ws, part, scale = v["hm"], v["hs"], v["wm"], v["ws"], v["part"], v["scale"]
    e_all, tcol, gcol, fcol, st1, st2 = v["e_all"], v["tcol"], v["gcol"], v["fcol"], v["st1"], v["st2"]

    def at_dp(yy, zz, cc):
        return (yy * 4 + zz * 2 + cc, pipe)

    def yo(o):
        return lax.rem(y + o + Y, Y)

    def block(o, zz):
        return yo(o) * 2 + zz

    def pipe_peer(i):
        return lax.rem(zh + i // 4, 4) * 4 + lax.rem(px + i % 4, 4)

    def dp_peer(i):
        return at_dp(lax.rem(y + i // 2, Y), lax.rem(zl + i % 2, 2), c)

    sib = at_dp(y, zl, 1 - c)
    zdev = at_dp(y, 1 - zl, c)
    pending = []

    def send(src, dst, s_sem, r_sem, dev):
        cp = pltpu.make_async_remote_copy(
            src_ref=src, dst_ref=dst, send_sem=s_sem, recv_sem=r_sem, device_id=dev, device_id_type=MESH
        )
        cp.start()
        return cp

    def push(src, dst, name, i, dev):
        cp = send(src, dst, s[name + "_s"].at[i], s[name + "_r"].at[i], dev)
        pending.append(cp)
        return cp

    def landed(ref, sem):
        pltpu.make_async_copy(ref, ref, sem).wait()

    local = [
        pltpu.make_async_copy(src, dst, s["local"].at[i])
        for i, (src, dst) in enumerate(((h_ref, hm.at[pipe]), (t_ref, v["t"]), (g_ref, v["g"]), (w_ref, wm)))
    ]
    for cp in local:
        cp.start()

    barrier = pltpu.get_barrier_semaphore()

    @pl.loop(1, 16)
    def _(i):
        pl.semaphore_signal(barrier, inc=1, device_id=(me_dp, pipe_peer(16 - i)), device_id_type=MESH)
        pl.semaphore_signal(barrier, inc=1, device_id=dp_peer(i), device_id_type=MESH)

    pl.semaphore_signal(barrier, inc=1, device_id=sib, device_id_type=MESH)
    for cp in local[:3]:
        cp.wait()
    pl.semaphore_wait(barrier, 31)

    @pl.loop(1, 16)
    def _(i):
        send(hm.at[pipe], hm.at[pipe], s["h_s"], s["h_r"].at[i // 4], (me_dp, pipe_peer(i)))

    half_rows = pl.ds(pl.multiple_of((1 - c) * HALF, HALF), HALF)
    w_swap = push(w_ref.at[half_rows], ws, "w", 0, sib)

    shape = (NB, ROWS, 128)
    b_id, r_id = lax.broadcasted_iota(I32, shape, 0), lax.broadcasted_iota(I32, shape, 1)
    pick = lax.broadcasted_iota(I32, shape, 2) == b_id * 8 + r_id % 8
    first = r_id < 8

    def column(ref):
        x = ref[...].astype(F32)
        x = jnp.where(first, x[0:1].reshape(1, 1, 128), x[1:2].reshape(1, 1, 128))
        return jnp.broadcast_to(jnp.sum(jnp.where(pick, x, 0.0), axis=-1, keepdims=True), shape)

    tcol[...] = column(v["t"]).astype(I32)
    gcol[...] = column(v["g"])

    full = (NB * ROWS, CHUNK)

    def twice(x):
        x = x.reshape(NB * ROWS, 128)
        return jnp.concatenate([x, x], axis=1)

    def at_target(q):
        ids = pipe * (2 * HALF) + q * CHUNK + lax.broadcasted_iota(I32, full, 1)
        return ids == twice(tcol[...])

    local[3].wait()
    v["wt"][...] = jnp.zeros(full, F32)

    @pl.loop(0, 2 * HALF // CHUNK)
    def _(q):
        cols = pl.ds(pl.multiple_of(q * CHUNK, CHUNK), CHUNK)
        one = jnp.where(at_target(q), 1.0, 0.0).astype(BF16)
        v["wt"][...] += jnp.dot(one, wm[cols, :], preferred_element_type=F32)

    near_first = (0, 1, 3, 2)
    forwards = []
    for n, dz in enumerate(near_first):
        group = pl.ds(lax.rem(zh + 4 - dz, 4) * 4, 4)
        landed(hm.at[pl.ds(0, 3 if dz == 0 else 4)], s["h_r"].at[dz])
        forwards.append(push(hm.at[group], hs.at[group], "hf", n, sib))
    for cp in forwards:
        cp.wait_recv()
    w_swap.wait_recv()

    nt = (((1,), (1,)), ((), ()))

    def products(u):
        scale[u] = jnp.zeros(shape, F32)

        @pl.loop(0, SUB // CHUNK)
        def _(k):
            k = u * (SUB // CHUNK) + k
            own = pl.ds(pl.multiple_of(c * HALF + k * CHUNK, CHUNK), CHUNK)
            there = pl.ds(pl.multiple_of(k * CHUNK, CHUNK), CHUNK)
            x = lax.dot_general(hm[...].reshape(full), wm[own, :], nt, preferred_element_type=F32)
            x += lax.dot_general(hs[...].reshape(full), ws[there, :], nt, preferred_element_type=F32)
            x = x.reshape(NB, ROWS, CHUNK)
            part[:, :, there] = x
            scale[u] = jnp.maximum(scale[u], jnp.maximum(jnp.abs(x[..., :128]), jnp.abs(x[..., 128:])))

        scale[u] = jnp.broadcast_to(jnp.max(scale[u], axis=-1, keepdims=True), shape)

    def lanes(u):
        return slice(u * SUB, (u + 1) * SUB)

    z_way = {}

    def z_issue():
        for n, o in enumerate(ORDER):
            b = block(o * SIGNS[0], 1 - zl)
            encode(v["zs"], n, part[b, :, lanes(0)], scale[0, b])
            z_way[o] = push(v["zs"].at[n], v["zr"].at[n], "z", n, zdev)

    def get(u, o):
        if u == 0:
            b = block(o * SIGNS[0], zl)
            z_way[o].wait_recv()
            x, bound = decode(v["zr"], ORDER.index(o))
            return part[b, :, lanes(0)] + x, scale[0, b] + bound
        pair = pl.ds(block(o * SIGNS[1], 0), 2)
        return part[pair, :, lanes(1)].reshape(2 * ROWS, SUB), scale[1, pair].reshape(2 * ROWS, 128)

    y_way = {}

    def add(u, got, *slots):
        x, bound = got
        for i in slots:
            y_way[u, i].wait_recv()
            more, more_bound = decode(v[f"yr{u}"], i)
            x, bound = x + more, bound + more_bound
        return x, bound

    def y_push(u, i, got):
        encode(v[f"ys{u}"], i, *got)
        dev = at_dp(yo(SIGNS[u] * WAYS[i][1]), zl, c)
        y_way[u, i] = push(v[f"ys{u}"].at[i], v[f"yr{u}"].at[i], f"y{u}", i, dev)

    def rs_first(u):
        for i in (0, 1, 2):
            y_push(u, i, get(u, WAYS[i][0]))

    def rs_near(u):
        for i in (3, 4):
            y_push(u, i, get(u, WAYS[i][0]))

    def rs_mid(u):
        y_push(u, 5, add(u, get(u, 2), 0, 1))
        y_push(u, 6, add(u, get(u, -2), 2))

    def rs_end(u):
        return add(u, get(u, 0), 3, 4, 5, 6)

    def rs_pair():
        x, bound = rs_end(1)
        v["xb"][...] = x.reshape(2, ROWS, SUB)
        v["sb"][...] = bound.reshape(2, ROWS, 128)
        encode(v["zs"], 8, v["xb"][1 - zl], v["sb"][1 - zl])
        z_way["pair"] = push(v["zs"].at[8], v["zr"].at[8], "z", 8, zdev)

    def rs_pair_end():
        z_way["pair"].wait_recv()
        return v["xb"][zl] + decode(v["zr"], 8)[0]

    wide = (ROWS, 128)

    def softmax(u, x):
        m_col = jnp.max(x, axis=1, keepdims=True)
        e = jnp.exp(x - m_col)
        s_col = jnp.sum(e, axis=1, keepdims=True)
        ids = pipe * (2 * HALF) + c * HALF + u * SUB + lax.broadcasted_iota(I32, x.shape, 1)
        hit = ids == jnp.concatenate([tcol[mb]] * (SUB // 128), axis=1)
        p_col = jnp.sum(jnp.where(hit, x, 0.0), axis=1, keepdims=True)
        e_all[c, u, mb] = jnp.where(hit, 0.0, e).astype(BF16)
        return [to_lanes(jnp.broadcast_to(a, wide)) for a in (m_col, s_col, p_col)]

    def chunk(u, b):
        return e_all.at[c, u, b]

    def ag_y(u, i, o, hop):
        b = block(o * SIGNS[u], zl)
        push(chunk(u, b), chunk(u, b), f"ay{u}", i, at_dp(yo(SIGNS[u] * hop), zl, c))

    def to_core(u, b):
        send(chunk(u, b), chunk(u, b), s["ac_s"], s["ac_r"].at[u], sib)

    def share(u, o):
        b = block(o * SIGNS[u], zl)
        push(chunk(u, b), chunk(u, b), f"az{u}", ORDER.index(o), zdev)
        to_core(u, b)

    def got_y(u, i, o):
        landed(chunk(u, block(o * SIGNS[u], zl)), s[f"ay{u}_r"].at[i])

    def got_z(u, *offsets):
        for o in offsets:
            b = block(o * SIGNS[u], 1 - zl)
            landed(chunk(u, b), s[f"az{u}_r"].at[ORDER.index(o)])
            to_core(u, b)

    def ag_own(u):
        for i, hop in ((1, 2), (3, -2), (0, 1), (2, -1)):
            ag_y(u, i, 0, hop)
        share(u, 0)

    def ag_near(u):
        got_y(u, 0, -1)
        share(u, -1)
        got_y(u, 2, 1)
        share(u, 1)
        got_y(u, 1, -2)
        ag_y(u, 5, -2, 2)
        ag_y(u, 4, -2, 1)
        share(u, -2)
        got_y(u, 3, 2)
        ag_y(u, 6, 2, -1)
        share(u, 2)

    def ag_far(u):
        for i, o in ((4, -3), (6, 3), (5, 4)):
            got_y(u, i, o)
            share(u, o)

    def weigh(u):
        landed(e_all.at[1 - c, u], s["ac_r"].at[u])
        for half in range(2):
            rows = slice(half * HALF + u * SUB, half * HALF + (u + 1) * SUB)
            e = e_all[half, u].reshape(NB * ROWS, SUB)
            v["acc"][half * 2 + u] = jnp.dot(e, wm[rows, :], preferred_element_type=F32)

    products(0)
    z_issue()
    products(1)
    rs_first(1)
    rs_near(1)
    rs_first(0)
    rs_near(0)
    rs_mid(1)
    rs_mid(0)
    rs_pair()
    stats0 = softmax(0, rs_end(0)[0])
    ag_own(0)
    stats1 = softmax(1, rs_pair_end())
    ag_own(1)

    def put(ref, rows):
        for n, row in enumerate(rows):
            ref[:, n * 128 : (n + 1) * 128] = row

    m_own = jnp.maximum(stats0[0], stats1[0])
    s_own = stats0[1] * jnp.exp(stats0[0] - m_own) + stats1[1] * jnp.exp(stats1[0] - m_own)
    put(v["mine"].at[0], (m_own, s_own, stats0[2] + stats1[2], stats0[0], stats1[0]))
    both = push(v["mine"].at[0], v["st0"].at[0], "st0", 0, sib)
    ag_near(0)
    both.wait_recv()
    other = [v["st0"][0, :, n * 128 : (n + 1) * 128] for n in range(5)]
    m_two = jnp.maximum(m_own, other[0])
    s_two = s_own * jnp.exp(m_own - m_two) + other[1] * jnp.exp(other[0] - m_two)
    put(st1.at[pipe], (m_two, s_two, stats0[2] + stats1[2] + other[2]))

    @pl.loop(1, 16)
    def _(i):
        send(st1.at[pipe], st1.at[pipe], s["st_s"].at[0], s["st_r"].at[0], (me_dp, pipe_peer(i)))

    ag_near(1)
    got_z(0, 0)
    ag_far(0)
    got_z(0, -1, 1)
    got_z(1, 0)
    ag_far(1)

    fifteen = st1.at[pl.ds(0, 15)]
    landed(fifteen, s["st_r"].at[0])
    ms, sums, picks = (st1[:, 0, n * 128 : (n + 1) * 128] for n in range(3))
    top = jnp.max(ms, axis=0, keepdims=True)
    total = jnp.sum(sums * jnp.exp(ms - top), axis=0, keepdims=True)
    picked = jnp.sum(picks, axis=0, keepdims=True)
    total = jnp.where(lax.broadcasted_iota(I32, (1, 128), 1) < ROWS, total, 1.0)
    g = to_lanes(gcol[mb])
    f_own = [g * (jnp.exp(st[0] - top) / total) for st in (stats0, stats1)]
    f_other = [g * (jnp.exp(m - top) / total) for m in other[3:]]
    at_hit = g * (jnp.exp(picked - top) / total - 1.0)
    loss = top + jnp.log(total) - picked
    low = [jnp.where(c == 0, a, b) for a, b in zip(f_own, f_other)]
    high = [jnp.where(c == 0, b, a) for a, b in zip(f_own, f_other)]
    put(st2.at[mb], (*low, *high, at_hit))

    @pl.loop(1, 16)
    def _(i):
        send(st2.at[mb], st2.at[mb], s["st_s"].at[1], s["st_r"].at[1], dp_peer(i))

    got_z(0, -2, 2)
    got_z(0, -3, 3, 4)
    got_z(1, -1, 1, -2, 2)
    weigh(0)
    loss_col = to_rows(loss)
    r2, l2 = lax.broadcasted_iota(I32, wide, 0), lax.broadcasted_iota(I32, wide, 1)
    loss_out = jnp.where(r2 % 8 == 4 * c + l2, loss_col, 0.0).reshape(2, 8, 128)
    v["loss"][...] = jnp.sum(loss_out, axis=1)
    got_z(1, -3, 3, 4)
    fifteen2 = st2.at[pl.ds(0, 15)]
    landed(fifteen2, s["st_r"].at[1])
    for n in range(5):
        fcol[n] = to_rows(st2[:, :, n * 128 : (n + 1) * 128])
    weigh(1)

    bound = 0.51 * jnp.abs(fcol[4]) + 1e-6 * gcol[...]
    dh = v["wt"][...] * twice(fcol[4])
    for n in range(4):
        dh += v["acc"][n] * twice(fcol[n])
    q16 = jnp.clip(dh * twice(TOP / bound), -TOP, TOP)
    v["dhs"][...] = jnp.round(q16).astype(I32).astype(I16).reshape(NB, ROWS, CHUNK)

    @pl.loop(1, 16)
    def _(i):
        to = pipe_peer(i)
        send(v["dhs"].at[to], v["dhr"].at[pipe], s["d_s"], s["d_r"], (me_dp, to))

    tn = (((0,), (0,)), ((), ()))

    @pl.loop(0, 2 * HALF // CHUNK)
    def _(q):
        hh, u, k = q // 8, (q // 4) % 2, q % 4
        e = e_all[hh, u, :, :, pl.ds(pl.multiple_of(k * CHUNK, CHUNK), CHUNK)].reshape(full).astype(F32)
        d = jnp.where(at_target(q), twice(fcol[4]), e * twice(fcol[hh * 2 + u])).astype(BF16)
        x = lax.dot_general(d, hm[...].reshape(full), tn, preferred_element_type=F32)
        rows = pl.ds(pl.multiple_of(q * CHUNK, CHUNK), CHUNK)
        v["dw"][rows, :] = x.astype(BF16)
        pltpu.make_async_copy(v["dw"].at[rows], dw_ref.at[rows], s["dw"]).start()

    v["dhr"][pipe] = v["dhs"][pipe]
    got15 = v["dhr"].at[pl.ds(0, 15)]
    landed(got15, s["d_r"])
    dh = jnp.sum(v["dhr"][...].astype(I32).astype(F32), axis=0)
    own_bound = 0.51 * jnp.abs(fcol[4, pipe]) + 1e-6 * gcol[pipe]
    v["dh"][...] = lanes_mul(dh, own_bound * (1.0 / TOP)).astype(BF16)
    outs = [
        pltpu.make_async_copy(src, dst, s["local"].at[i])
        for i, (src, dst) in enumerate(((v["dh"], dh_ref), (v["loss"], loss_ref)))
    ]
    for cp in outs:
        cp.start()

    for cp in pending:
        cp.wait_send()
    landed(hm.at[pl.ds(0, 15)], s["h_s"])
    landed(fifteen, s["st_s"].at[0])
    landed(fifteen2, s["st_s"].at[1])
    landed(e_all.at[c], s["ac_s"])
    landed(got15, s["d_s"])
    pltpu.make_async_copy(v["dw"], dw_ref, s["dw"]).wait()
    for cp in outs:
        cp.wait()


def call(hidden, weight, targets, row_grad):
    dma, vm = pltpu.SemaphoreType.DMA, pltpu.VMEM
    one, two = (ROWS, SUB + CODE), (2 * ROWS, SUB + CODE)
    hbm = pl.BlockSpec(memory_space=pltpu.HBM)
    buffers = dict(
        hm=vm((NB, ROWS, CHUNK), BF16), hs=vm((NB, ROWS, CHUNK), BF16),
        wm=vm((2 * HALF, CHUNK), BF16), ws=vm((HALF, CHUNK), BF16),
        part=vm((NB, ROWS, HALF), F32), scale=vm((NSUB, NB, ROWS, 128), F32),
        t=vm((2, 128), I32), g=vm((2, 128), F32), tcol=vm((NB, ROWS, 128), I32), gcol=vm((NB, ROWS, 128), F32),
        wt=vm((NB * ROWS, CHUNK), F32), acc=vm((4, NB * ROWS, CHUNK), F32), fcol=vm((5, NB, ROWS, 128), F32),
        e_all=vm((2, NSUB, NB, ROWS, SUB), BF16), dw=vm((2 * HALF, CHUNK), BF16),
        zs=vm((9,) + one, I16), zr=vm((9,) + one, I16), ys0=vm((7,) + one, I16), yr0=vm((7,) + one, I16),
        ys1=vm((7,) + two, I16), yr1=vm((7,) + two, I16), xb=vm((2, ROWS, SUB), F32), sb=vm((2, ROWS, 128), F32),
        mine=vm((1, 1, 640), F32), st0=vm((1, 1, 640), F32), st1=vm((NB, 1, 384), F32), st2=vm((NB, 1, 640), F32),
        dhs=vm((NB, ROWS, CHUNK), I16), dhr=vm((NB, ROWS, CHUNK), I16), dh=vm((ROWS, CHUNK), BF16),
        loss=vm((2, 128), F32),
    )
    pairs = dict(w=1, hf=4, z=9, y0=7, y1=7, ay0=7, ay1=7, az0=8, az1=8, st0=1, st=2)
    sems = dict(
        local=dma((4,)), h_s=dma, h_r=dma((4,)), ac_s=dma, ac_r=dma((2,)), d_s=dma, d_r=dma, dw=dma,
        **{name + end: dma((n,)) for name, n in pairs.items() for end in ("_s", "_r")},
    )
    return pl.pallas_call(
        kernel,
        out_shape=(
            jax.ShapeDtypeStruct((ROWS, CHUNK), BF16),
            jax.ShapeDtypeStruct((2 * HALF, CHUNK), BF16),
            jax.ShapeDtypeStruct((2, 128), F32),
        ),
        in_specs=[hbm] * 4,
        out_specs=(hbm,) * 3,
        scratch_shapes=(buffers, sems),
        compiler_params=pltpu.CompilerParams(
            collective_id=0, has_side_effects=True, vmem_limit_bytes=60 << 20
        ),
        cost_estimate=pl.CostEstimate(flops=1_600_000_000, bytes_accessed=5 << 20, transcendentals=1 << 20),
        name="output_layer",
    )(hidden, weight, targets, row_grad)


PIECES = 8


def settle(dh, dw, loss, dh_out, dw_out, loss_out, dh_v, dw_v, loss_v, sem_in, sem_out):
    rows = 2 * HALF // PIECES
    moves = [(dh, dh_v, dh_out), (loss, loss_v, loss_out)]
    for i in range(PIECES):
        at = pl.ds(i * rows, rows)
        moves.append((dw.at[at], dw_v.at[at], dw_out.at[at]))
    into = [pltpu.make_async_copy(a, b, sem_in.at[i]) for i, (a, b, _) in enumerate(moves)]
    out = [pltpu.make_async_copy(b, d, sem_out.at[i]) for i, (_, b, d) in enumerate(moves)]
    for cp in into:
        cp.start()
    for cp, then in zip(into, out):
        cp.wait()
        then.start()
    for cp in out:
        cp.wait()


def on_device(hidden, weight, targets, row_grad):
    found = call(hidden.reshape(ROWS, CHUNK), weight, targets, row_grad)
    hbm = pl.BlockSpec(memory_space=pltpu.HBM)
    grad_hidden, grad_weight, row_loss = pl.pallas_call(
        settle,
        out_shape=[jax.ShapeDtypeStruct(x.shape, x.dtype) for x in found],
        in_specs=[hbm] * 3,
        out_specs=[hbm] * 3,
        scratch_shapes=[pltpu.VMEM(x.shape, x.dtype) for x in found]
        + [pltpu.SemaphoreType.DMA((PIECES + 2,)), pltpu.SemaphoreType.DMA((PIECES + 2,))],
        compiler_params=pltpu.CompilerParams(vmem_limit_bytes=60 << 20),
        name="settle",
    )(*found)
    return grad_hidden.reshape(2, 8, CHUNK), grad_weight, row_loss[:, :4]


def solution(mesh):
    placed = (P(None, "pipe", "dp"), P("pipe", "dp"), P(), P())
    return jax.shard_map(
        on_device,
        mesh=mesh,
        in_specs=placed,
        out_specs=(P(None, "pipe", "dp"), P("pipe", "dp"), P(None, "dp")),
        check_vma=False,
    )
```

time: 756 us -> 71 us (0.09)
  waiting for transfers between devices: 569 us -> 0 us
  blocking collectives: 144 us -> 0 us
  Pallas kernels: 0 us -> 69.3 us
  matrix products: 14.9 us -> 0 us
  between operations: 14.5 us -> 0.64 us
    unnamed x6 -> x0, waiting for transfers between devices: 253 us -> none
    reduce_scatter x2 -> x0, waiting for transfers between devices: 175 us -> none  [on_device(): lax.psum_scatter(jnp.dot(dl_all, weight, preferred_element_type=jnp.float...]
    all_gather x2 -> x0, waiting for transfers between devices: 140 us -> none  [on_device(): dl_all = lax.all_gather(dlogits, 'dp', axis=0, tiled=True)]
    all_gather x2 -> x0, blocking collectives: 74.4 us -> none  [on_device(): h_full = lax.all_gather(hidden[micro], 'pipe', axis=0, tiled=True)]
    pallas_call x0 -> x2, Pallas kernels: none -> 69.3 us  [the longest x1 66.8 us: call(): pl.pallas_call(kernel, out_shape=(jax.ShapeDtypeStruct((ROWS, CHUNK), BF1...]
    pmax x1 -> x0, blocking collectives: 36.9 us -> none  [on_device(): top = lax.pmax(local_max, 'pipe')]
    psum x1 -> x0, blocking collectives: 32.4 us -> none  [on_device(): lax.psum((jnp.sum(jnp.exp(logits - top[:, None]), axis=1), picked_part),...]
    dot_general x6 -> x0, matrix products: 14.9 us -> none  [the longest x2 7.23 us: on_device(): lax.dot_general(dl_all, h_full, (((0,), (0,)), ((), ())), preferred_eleme...]
  transfers between devices with their start and end apart: 5 -> 0, of which waited for: 5 -> 0; matrix products, arithmetic and copies ran while one was open for 2% -> 0% of each run, Pallas kernels for 0% -> 0%
where the time goes in v2:
time: 71 us; the launch traced here: 69.9 us
  Pallas kernels  69.3 us (98%)
    pallas_call x1, Pallas kernels, call(): pl.pallas_call(kernel, out_shape=(jax.ShapeDtypeStruct((ROWS, CHUNK), BF1...  66.8 us
    pallas_call x1, Pallas kernels, on_device(): pl.pallas_call(settle, out_shape=[jax.ShapeDtypeStruct(x.shape, x.dtype)...  2.45 us

profile of v2, /device:TPU:1, one launch (start us, length us, event | category | flops | bytes accessed | tf_op | source)
XLA Modules:
  0.0 69.9 jit_solution(6187939377680183666)
XLA Ops:
  0.6 66.8 %output_layer.1 = (bf16[16,256]{1,0:T(8,128)(2,1)}, bf16[4096,256]{1,0:T(8,128)(2,1)}, f32[2,128]{1,0:T(2,128)}) custom-call(bf16[16,256]{1,0:T(8,128)(2,1)} %bitcast.3, bf16[4096,256]{1,0:T(8,128)(2,1)} %w_ref.1, s32[2,128]{1,0:T(2,128)} %t_ref.1, f32[2,128]{1,0:T(2,128)} %g_ref.1), custom_call_target="tpu_custom_call" | custom-call | flops 1600000000 | bytes 5242880 | tf_op jit(solution)/shard_map/output_layer/pallas_call | solution.py:470
  67.5 2.5 %settle.1 = (bf16[16,256]{1,0:T(8,128)(2,1)}, bf16[4096,256]{1,0:T(8,128)(2,1)}, f32[2,128]{1,0:T(2,128)}) custom-call(bf16[16,256]{1,0:T(8,128)(2,1)} %get-tuple-element.9.dh, bf16[4096,256]{1,0:T(8,128)(2,1)} %get-tuple-element.10.dw, f32[2,128]{1,0:T(2,128)} %get-tuple-element.11.loss), custom_call_target="tpu_custom_call" | custom-call | tf_op jit(solution)/shard_map/settle/pallas_call | solution.py:511

commit v3 on v2

--- a/solution.py
+++ b/solution.py
@@ -61,7 +61,8 @@
 
 
 WAYS = ((4, 2), (3, 1), (-3, -1), (1, 1), (-1, -1), (2, 2), (-2, -2))
-ORDER = (4, 3, -3, 2, -2, 1, -1, 0)
+CROSS = (4, 3, -3, 2, -2, 0)
+WIDTHS = dict(z=6, x=2, y=7)
 SIGNS = (1, -1)
 
 
@@ -82,6 +83,9 @@
     def block(o, zz):
         return yo(o) * 2 + zz
 
+    def far_first(j):
+        return lax.rem(j + 7, 15) + 1
+
     def pipe_peer(i):
         return lax.rem(zh + i // 4, 4) * 4 + lax.rem(px + i % 4, 4)
 
@@ -116,9 +120,10 @@
 
     barrier = pltpu.get_barrier_semaphore()
 
-    @pl.loop(1, 16)
-    def _(i):
-        pl.semaphore_signal(barrier, inc=1, device_id=(me_dp, pipe_peer(16 - i)), device_id_type=MESH)
+    @pl.loop(0, 15)
+    def _(j):
+        i = far_first(j)
+        pl.semaphore_signal(barrier, inc=1, device_id=(me_dp, pipe_peer(i)), device_id_type=MESH)
         pl.semaphore_signal(barrier, inc=1, device_id=dp_peer(i), device_id_type=MESH)
 
     pl.semaphore_signal(barrier, inc=1, device_id=sib, device_id_type=MESH)
@@ -126,8 +131,9 @@
         cp.wait()
     pl.semaphore_wait(barrier, 31)
 
-    @pl.loop(1, 16)
-    def _(i):
+    @pl.loop(0, 15)
+    def _(j):
+        i = far_first(j)
         send(hm.at[pipe], hm.at[pipe], s["h_s"], s["h_r"].at[i // 4], (me_dp, pipe_peer(i)))
 
     half_rows = pl.ds(pl.multiple_of((1 - c) * HALF, HALF), HALF)
@@ -180,11 +186,9 @@
     def products(u):
         scale[u] = jnp.zeros(shape, F32)
 
-        @pl.loop(0, SUB // CHUNK)
-        def _(k):
-            k = u * (SUB // CHUNK) + k
+        for k in range(u * SUB // CHUNK, (u + 1) * SUB // CHUNK):
             own = pl.ds(pl.multiple_of(c * HALF + k * CHUNK, CHUNK), CHUNK)
-            there = pl.ds(pl.multiple_of(k * CHUNK, CHUNK), CHUNK)
+            there = pl.ds(k * CHUNK, CHUNK)
             x = lax.dot_general(hm[...].reshape(full), wm[own, :], nt, preferred_element_type=F32)
             x += lax.dot_general(hs[...].reshape(full), ws[there, :], nt, preferred_element_type=F32)
             x = x.reshape(NB, ROWS, CHUNK)
@@ -196,63 +200,56 @@
     def lanes(u):
         return slice(u * SUB, (u + 1) * SUB)
 
-    z_way = {}
-
-    def z_issue():
-        for n, o in enumerate(ORDER):
-            b = block(o * SIGNS[0], 1 - zl)
-            encode(v["zs"], n, part[b, :, lanes(0)], scale[0, b])
-            z_way[o] = push(v["zs"].at[n], v["zr"].at[n], "z", n, zdev)
-
-    def get(u, o):
-        if u == 0:
-            b = block(o * SIGNS[0], zl)
-            z_way[o].wait_recv()
-            x, bound = decode(v["zr"], ORDER.index(o))
-            return part[b, :, lanes(0)] + x, scale[0, b] + bound
-        pair = pl.ds(block(o * SIGNS[1], 0), 2)
-        return part[pair, :, lanes(1)].reshape(2 * ROWS, SUB), scale[1, pair].reshape(2 * ROWS, 128)
-
-    y_way = {}
-
-    def add(u, got, *slots):
+    def own(u, b):
+        return part[b, :, lanes(u)], scale[u, b]
+
+    way = {}
+
+    def go(u, name, i, got, dev):
+        encode(v[f"{name}s"], u * WIDTHS[name] + i, *got)
+        slot = u * WIDTHS[name] + i
+        way[name, u, i] = push(v[f"{name}s"].at[slot], v[f"{name}r"].at[slot], name, slot, dev)
+
+    def add(u, got, name, *slots):
         x, bound = got
         for i in slots:
-            y_way[u, i].wait_recv()
-            more, more_bound = decode(v[f"yr{u}"], i)
+            way[name, u, i].wait_recv()
+            more, more_bound = decode(v[f"{name}r"], u * WIDTHS[name] + i)
             x, bound = x + more, bound + more_bound
         return x, bound
 
-    def y_push(u, i, got):
-        encode(v[f"ys{u}"], i, *got)
-        dev = at_dp(yo(SIGNS[u] * WAYS[i][1]), zl, c)
-        y_way[u, i] = push(v[f"ys{u}"].at[i], v[f"yr{u}"].at[i], f"y{u}", i, dev)
+    def at_y(u, hop):
+        return at_dp(yo(SIGNS[u] * hop), zl, c)
+
+    def rs_z(u, *offsets):
+        for o in offsets:
+            go(u, "z", CROSS.index(o), own(u, block(o * SIGNS[u], 1 - zl)), zdev)
+
+    def rs_side(u):
+        for i, o in enumerate((1, -1)):
+            go(u, "x", i, own(u, block(o * SIGNS[u], 1 - zl)), at_y(u, o))
+
+    def rs_near(u):
+        for i in (3, 4):
+            o, hop = WAYS[i]
+            go(u, "y", i, own(u, block(o * SIGNS[u], zl)), at_y(u, hop))
+
+    def rs_z_own(u):
+        go(u, "z", 5, add(u, own(u, block(0, 1 - zl)), "x", 0, 1), zdev)
+
+    def crossed(u, o):
+        return add(u, own(u, block(o * SIGNS[u], zl)), "z", CROSS.index(o))
 
     def rs_first(u):
         for i in (0, 1, 2):
-            y_push(u, i, get(u, WAYS[i][0]))
-
-    def rs_near(u):
-        for i in (3, 4):
-            y_push(u, i, get(u, WAYS[i][0]))
+            go(u, "y", i, crossed(u, WAYS[i][0]), at_y(u, WAYS[i][1]))
 
     def rs_mid(u):
-        y_push(u, 5, add(u, get(u, 2), 0, 1))
-        y_push(u, 6, add(u, get(u, -2), 2))
+        go(u, "y", 5, add(u, crossed(u, 2), "y", 0, 1), at_y(u, 2))
+        go(u, "y", 6, add(u, crossed(u, -2), "y", 2), at_y(u, -2))
 
     def rs_end(u):
-        return add(u, get(u, 0), 3, 4, 5, 6)
-
-    def rs_pair():
-        x, bound = rs_end(1)
-        v["xb"][...] = x.reshape(2, ROWS, SUB)
-        v["sb"][...] = bound.reshape(2, ROWS, 128)
-        encode(v["zs"], 8, v["xb"][1 - zl], v["sb"][1 - zl])
-        z_way["pair"] = push(v["zs"].at[8], v["zr"].at[8], "z", 8, zdev)
-
-    def rs_pair_end():
-        z_way["pair"].wait_recv()
-        return v["xb"][zl] + decode(v["zr"], 8)[0]
+        return add(u, crossed(u, 0), "y", 3, 4, 5, 6)[0]
 
     wide = (ROWS, 128)
 
@@ -266,52 +263,63 @@
         e_all[c, u, mb] = jnp.where(hit, 0.0, e).astype(BF16)
         return [to_lanes(jnp.broadcast_to(a, wide)) for a in (m_col, s_col, p_col)]
 
-    def chunk(u, b):
-        return e_all.at[c, u, b]
-
-    def ag_y(u, i, o, hop):
-        b = block(o * SIGNS[u], zl)
-        push(chunk(u, b), chunk(u, b), f"ay{u}", i, at_dp(yo(SIGNS[u] * hop), zl, c))
-
-    def to_core(u, b):
-        send(chunk(u, b), chunk(u, b), s["ac_s"], s["ac_r"].at[u], sib)
-
-    def share(u, o):
-        b = block(o * SIGNS[u], zl)
-        push(chunk(u, b), chunk(u, b), f"az{u}", ORDER.index(o), zdev)
-        to_core(u, b)
-
-    def got_y(u, i, o):
-        landed(chunk(u, block(o * SIGNS[u], zl)), s[f"ay{u}_r"].at[i])
-
-    def got_z(u, *offsets):
-        for o in offsets:
-            b = block(o * SIGNS[u], 1 - zl)
-            landed(chunk(u, b), s[f"az{u}_r"].at[ORDER.index(o)])
-            to_core(u, b)
+    def chunk(u, o, side=0):
+        return e_all.at[c, u, block(o * SIGNS[u], zl if side == 0 else 1 - zl)]
+
+    def to_core(u, ref):
+        send(ref, ref, s["ac_s"], s["ac_r"].at[u], sib)
+
+    def ag(u, name, i, ref, dev):
+        push(ref, ref, "a" + name, u * WIDTHS[name] + i, dev)
+
+    def got(u, name, i, ref):
+        landed(ref, s[f"a{name}_r"].at[u * WIDTHS[name] + i])
+
+    def cross(u, o):
+        ag(u, "z", CROSS.index(o), chunk(u, o), zdev)
 
     def ag_own(u):
+        ref = chunk(u, 0)
+        cross(u, 0)
         for i, hop in ((1, 2), (3, -2), (0, 1), (2, -1)):
-            ag_y(u, i, 0, hop)
-        share(u, 0)
+            ag(u, "y", i, ref, at_y(u, hop))
+        to_core(u, ref)
+
+    def ag_side(u):
+        ref = chunk(u, 0, 1)
+        got(u, "z", 5, ref)
+        for i, hop in enumerate((1, -1)):
+            ag(u, "x", i, ref, at_y(u, hop))
+        to_core(u, ref)
 
     def ag_near(u):
-        got_y(u, 0, -1)
-        share(u, -1)
-        got_y(u, 2, 1)
-        share(u, 1)
-        got_y(u, 1, -2)
-        ag_y(u, 5, -2, 2)
-        ag_y(u, 4, -2, 1)
-        share(u, -2)
-        got_y(u, 3, 2)
-        ag_y(u, 6, 2, -1)
-        share(u, 2)
+        got(u, "y", 1, chunk(u, -2))
+        ag(u, "y", 5, chunk(u, -2), at_y(u, 2))
+        ag(u, "y", 4, chunk(u, -2), at_y(u, 1))
+        cross(u, -2)
+        got(u, "y", 3, chunk(u, 2))
+        ag(u, "y", 6, chunk(u, 2), at_y(u, -1))
+        cross(u, 2)
+        for i, o in ((0, -1), (2, 1)):
+            got(u, "y", i, chunk(u, o))
+        for o in (-2, 2, -1, 1):
+            to_core(u, chunk(u, o))
 
     def ag_far(u):
         for i, o in ((4, -3), (6, 3), (5, 4)):
-            got_y(u, i, o)
-            share(u, o)
+            got(u, "y", i, chunk(u, o))
+            cross(u, o)
+            to_core(u, chunk(u, o))
+
+    def ag_side_near(u):
+        for i, o in enumerate((-1, 1)):
+            got(u, "x", i, chunk(u, o, 1))
+            to_core(u, chunk(u, o, 1))
+
+    def ag_crossed(u, *offsets):
+        for o in offsets:
+            got(u, "z", CROSS.index(o), chunk(u, o, 1))
+            to_core(u, chunk(u, o, 1))
 
     def weigh(u):
         landed(e_all.at[1 - c, u], s["ac_r"].at[u])
@@ -321,18 +329,24 @@
             v["acc"][half * 2 + u] = jnp.dot(e, wm[rows, :], preferred_element_type=F32)
 
     products(0)
-    z_issue()
+    rs_z(0, 4, 3, -3)
+    rs_side(0)
     products(1)
+    rs_z(1, 4, 3, -3)
+    rs_side(1)
+    rs_z(0, 2, -2)
+    rs_z(1, 2, -2)
+    rs_first(0)
+    rs_near(0)
+    rs_z_own(0)
     rs_first(1)
     rs_near(1)
-    rs_first(0)
-    rs_near(0)
+    rs_z_own(1)
+    rs_mid(0)
     rs_mid(1)
-    rs_mid(0)
-    rs_pair()
-    stats0 = softmax(0, rs_end(0)[0])
+    stats0 = softmax(0, rs_end(0))
     ag_own(0)
-    stats1 = softmax(1, rs_pair_end())
+    stats1 = softmax(1, rs_end(1))
     ag_own(1)
 
     def put(ref, rows):
@@ -343,22 +357,24 @@
     s_own = stats0[1] * jnp.exp(stats0[0] - m_own) + stats1[1] * jnp.exp(stats1[0] - m_own)
     put(v["mine"].at[0], (m_own, s_own, stats0[2] + stats1[2], stats0[0], stats1[0]))
     both = push(v["mine"].at[0], v["st0"].at[0], "st0", 0, sib)
-    ag_near(0)
+    ag_side(0)
     both.wait_recv()
     other = [v["st0"][0, :, n * 128 : (n + 1) * 128] for n in range(5)]
     m_two = jnp.maximum(m_own, other[0])
     s_two = s_own * jnp.exp(m_own - m_two) + other[1] * jnp.exp(other[0] - m_two)
     put(st1.at[pipe], (m_two, s_two, stats0[2] + stats1[2] + other[2]))
 
-    @pl.loop(1, 16)
-    def _(i):
+    @pl.loop(0, 15)
+    def _(j):
+        i = far_first(j)
         send(st1.at[pipe], st1.at[pipe], s["st_s"].at[0], s["st_r"].at[0], (me_dp, pipe_peer(i)))
 
+    ag_near(0)
+    ag_side(1)
     ag_near(1)
-    got_z(0, 0)
+    ag_side_near(0)
     ag_far(0)
-    got_z(0, -1, 1)
-    got_z(1, 0)
+    ag_side_near(1)
     ag_far(1)
 
     fifteen = st1.at[pl.ds(0, 15)]
@@ -375,21 +391,22 @@
     loss = top + jnp.log(total) - picked
     low = [jnp.where(c == 0, a, b) for a, b in zip(f_own, f_other)]
     high = [jnp.where(c == 0, b, a) for a, b in zip(f_own, f_other)]
-    put(st2.at[mb], (*low, *high, at_hit))
-
-    @pl.loop(1, 16)
-    def _(i):
+    put(st2.at[mb], (*low, *high, at_hit.astype(BF16).astype(F32)))
+
+    @pl.loop(0, 15)
+    def _(j):
+        i = far_first(j)
         send(st2.at[mb], st2.at[mb], s["st_s"].at[1], s["st_r"].at[1], dp_peer(i))
 
-    got_z(0, -2, 2)
-    got_z(0, -3, 3, 4)
-    got_z(1, -1, 1, -2, 2)
+    ag_crossed(0, -2, 2)
+    ag_crossed(1, -2, 2)
+    ag_crossed(0, -3, 3, 4)
     weigh(0)
     loss_col = to_rows(loss)
     r2, l2 = lax.broadcasted_iota(I32, wide, 0), lax.broadcasted_iota(I32, wide, 1)
     loss_out = jnp.where(r2 % 8 == 4 * c + l2, loss_col, 0.0).reshape(2, 8, 128)
     v["loss"][...] = jnp.sum(loss_out, axis=1)
-    got_z(1, -3, 3, 4)
+    ag_crossed(1, -3, 3, 4)
     fifteen2 = st2.at[pl.ds(0, 15)]
     landed(fifteen2, s["st_r"].at[1])
     for n in range(5):
@@ -403,8 +420,9 @@
     q16 = jnp.clip(dh * twice(TOP / bound), -TOP, TOP)
     v["dhs"][...] = jnp.round(q16).astype(I32).astype(I16).reshape(NB, ROWS, CHUNK)
 
-    @pl.loop(1, 16)
-    def _(i):
+    @pl.loop(0, 15)
+    def _(j):
+        i = far_first(j)
         to = pipe_peer(i)
         send(v["dhs"].at[to], v["dhr"].at[pipe], s["d_s"], s["d_r"], (me_dp, to))
 
@@ -447,7 +465,7 @@
 
 def call(hidden, weight, targets, row_grad):
     dma, vm = pltpu.SemaphoreType.DMA, pltpu.VMEM
-    one, two = (ROWS, SUB + CODE), (2 * ROWS, SUB + CODE)
+    one = (ROWS, SUB + CODE)
     hbm = pl.BlockSpec(memory_space=pltpu.HBM)
     buffers = dict(
         hm=vm((NB, ROWS, CHUNK), BF16), hs=vm((NB, ROWS, CHUNK), BF16),
@@ -456,13 +474,13 @@
         t=vm((2, 128), I32), g=vm((2, 128), F32), tcol=vm((NB, ROWS, 128), I32), gcol=vm((NB, ROWS, 128), F32),
         wt=vm((NB * ROWS, CHUNK), F32), acc=vm((4, NB * ROWS, CHUNK), F32), fcol=vm((5, NB, ROWS, 128), F32),
         e_all=vm((2, NSUB, NB, ROWS, SUB), BF16), dw=vm((2 * HALF, CHUNK), BF16),
-        zs=vm((9,) + one, I16), zr=vm((9,) + one, I16), ys0=vm((7,) + one, I16), yr0=vm((7,) + one, I16),
-        ys1=vm((7,) + two, I16), yr1=vm((7,) + two, I16), xb=vm((2, ROWS, SUB), F32), sb=vm((2, ROWS, 128), F32),
+        **{name + end: vm((NSUB * n,) + one, I16) for name, n in WIDTHS.items() for end in "sr"},
         mine=vm((1, 1, 640), F32), st0=vm((1, 1, 640), F32), st1=vm((NB, 1, 384), F32), st2=vm((NB, 1, 640), F32),
         dhs=vm((NB, ROWS, CHUNK), I16), dhr=vm((NB, ROWS, CHUNK), I16), dh=vm((ROWS, CHUNK), BF16),
         loss=vm((2, 128), F32),
     )
-    pairs = dict(w=1, hf=4, z=9, y0=7, y1=7, ay0=7, ay1=7, az0=8, az1=8, st0=1, st=2)
+    pairs = dict(w=1, hf=4, st0=1, st=2)
+    pairs.update({a + name: NSUB * n for name, n in WIDTHS.items() for a in ("", "a")})
     sems = dict(
         local=dma((4,)), h_s=dma, h_r=dma((4,)), ac_s=dma, ac_r=dma((2,)), d_s=dma, d_r=dma, dw=dma,
         **{name + end: dma((n,)) for name, n in pairs.items() for end in ("_s", "_r")},

time: 71 us -> 66 us (0.930); the launches traced: 69.9 us -> 65.8 us
  Pallas kernels: 69.3 us -> 65.1 us
    pallas_call x1, Pallas kernels: 66.8 us -> 62.7 us  [call(): pl.pallas_call(kernel, out_shape=(jax.ShapeDtypeStruct((ROWS, CHUNK), BF1...]
where the time goes in v3:
time: 66 us; the launch traced here: 65.8 us
  Pallas kernels  65.1 us (99%)
    pallas_call x1, Pallas kernels, call(): pl.pallas_call(kernel, out_shape=(jax.ShapeDtypeStruct((ROWS, CHUNK), BF1...  62.7 us
    pallas_call x1, Pallas kernels, on_device(): pl.pallas_call(settle, out_shape=[jax.ShapeDtypeStruct(x.shape, x.dtype)...  2.45 us

profile of v3, /device:TPU:1, one launch (start us, length us, event | category | flops | bytes accessed | tf_op | source)
XLA Modules:
  0.0 65.8 jit_solution(3651985531503616874)
XLA Ops:
  0.6 62.7 %output_layer.1 = (bf16[16,256]{1,0:T(8,128)(2,1)}, bf16[4096,256]{1,0:T(8,128)(2,1)}, f32[2,128]{1,0:T(2,128)}) custom-call(bf16[16,256]{1,0:T(8,128)(2,1)} %bitcast.3, bf16[4096,256]{1,0:T(8,128)(2,1)} %w_ref.1, s32[2,128]{1,0:T(2,128)} %t_ref.1, f32[2,128]{1,0:T(2,128)} %g_ref.1), custom_call_target="tpu_custom_call" | custom-call | flops 1600000000 | bytes 5242880 | tf_op jit(solution)/shard_map/output_layer/pallas_call | solution.py:488
  63.3 2.5 %settle.1 = (bf16[16,256]{1,0:T(8,128)(2,1)}, bf16[4096,256]{1,0:T(8,128)(2,1)}, f32[2,128]{1,0:T(2,128)}) custom-call(bf16[16,256]{1,0:T(8,128)(2,1)} %get-tuple-element.9.dh, bf16[4096,256]{1,0:T(8,128)(2,1)} %get-tuple-element.10.dw, f32[2,128]{1,0:T(2,128)} %get-tuple-element.11.loss), custom_call_target="tpu_custom_call" | custom-call | tf_op jit(solution)/shard_map/settle/pallas_call | solution.py:529

commit v4 on v3

--- a/solution.py
+++ b/solution.py
@@ -177,25 +177,30 @@
         group = pl.ds(lax.rem(zh + 4 - dz, 4) * 4, 4)
         landed(hm.at[pl.ds(0, 3 if dz == 0 else 4)], s["h_r"].at[dz])
         forwards.append(push(hm.at[group], hs.at[group], "hf", n, sib))
+
+    nt = (((1,), (1,)), ((), ()))
+
+    def products(u, first):
+        if not first:
+            scale[u] = jnp.zeros(shape, F32)
+        for k in range(u * SUB // CHUNK, (u + 1) * SUB // CHUNK):
+            own = pl.ds(pl.multiple_of(c * HALF + k * CHUNK, CHUNK), CHUNK)
+            there = pl.ds(k * CHUNK, CHUNK)
+            held, rows = (hm, wm[own, :]) if first else (hs, ws[there, :])
+            x = lax.dot_general(held[...].reshape(full), rows, nt, preferred_element_type=F32)
+            x = x.reshape(NB, ROWS, CHUNK)
+            if not first:
+                x += part[:, :, there]
+                scale[u] = jnp.maximum(scale[u], jnp.maximum(jnp.abs(x[..., :128]), jnp.abs(x[..., 128:])))
+            part[:, :, there] = x
+        if not first:
+            scale[u] = jnp.broadcast_to(jnp.max(scale[u], axis=-1, keepdims=True), shape)
+
+    for u in range(NSUB):
+        products(u, True)
     for cp in forwards:
         cp.wait_recv()
     w_swap.wait_recv()
-
-    nt = (((1,), (1,)), ((), ()))
-
-    def products(u):
-        scale[u] = jnp.zeros(shape, F32)
-
-        for k in range(u * SUB // CHUNK, (u + 1) * SUB // CHUNK):
-            own = pl.ds(pl.multiple_of(c * HALF + k * CHUNK, CHUNK), CHUNK)
-            there = pl.ds(k * CHUNK, CHUNK)
-            x = lax.dot_general(hm[...].reshape(full), wm[own, :], nt, preferred_element_type=F32)
-            x += lax.dot_general(hs[...].reshape(full), ws[there, :], nt, preferred_element_type=F32)
-            x = x.reshape(NB, ROWS, CHUNK)
-            part[:, :, there] = x
-            scale[u] = jnp.maximum(scale[u], jnp.maximum(jnp.abs(x[..., :128]), jnp.abs(x[..., 128:])))
-
-        scale[u] = jnp.broadcast_to(jnp.max(scale[u], axis=-1, keepdims=True), shape)
 
     def lanes(u):
         return slice(u * SUB, (u + 1) * SUB)
@@ -328,19 +333,18 @@
             e = e_all[half, u].reshape(NB * ROWS, SUB)
             v["acc"][half * 2 + u] = jnp.dot(e, wm[rows, :], preferred_element_type=F32)
 
-    products(0)
+    products(0, False)
     rs_z(0, 4, 3, -3)
-    rs_side(0)
-    products(1)
+    products(1, False)
     rs_z(1, 4, 3, -3)
-    rs_side(1)
+    for u in range(NSUB):
+        rs_side(u)
+        rs_near(u)
     rs_z(0, 2, -2)
     rs_z(1, 2, -2)
     rs_first(0)
-    rs_near(0)
+    rs_first(1)
     rs_z_own(0)
-    rs_first(1)
-    rs_near(1)
     rs_z_own(1)
     rs_mid(0)
     rs_mid(1)

time: 66 us -> 64.5 us (0.977)
  Pallas kernels: 65.1 us -> 63.6 us
    pallas_call x1, Pallas kernels: 62.7 us -> 61.2 us  [call(): pl.pallas_call(kernel, out_shape=(jax.ShapeDtypeStruct((ROWS, CHUNK), BF1...]
where the time goes in v4:
time: 64.5 us; the launch traced here: 64.3 us
  Pallas kernels  63.6 us (99%)
    pallas_call x1, Pallas kernels, call(): pl.pallas_call(kernel, out_shape=(jax.ShapeDtypeStruct((ROWS, CHUNK), BF1...  61.2 us
    pallas_call x1, Pallas kernels, on_device(): pl.pallas_call(settle, out_shape=[jax.ShapeDtypeStruct(x.shape, x.dtype)...  2.45 us

profile of v4, /device:TPU:1, one launch (start us, length us, event | category | flops | bytes accessed | tf_op | source)
XLA Modules:
  0.0 64.3 jit_solution(13301508522849598778)
XLA Ops:
  0.6 61.2 %output_layer.1 = (bf16[16,256]{1,0:T(8,128)(2,1)}, bf16[4096,256]{1,0:T(8,128)(2,1)}, f32[2,128]{1,0:T(2,128)}) custom-call(bf16[16,256]{1,0:T(8,128)(2,1)} %bitcast.3, bf16[4096,256]{1,0:T(8,128)(2,1)} %w_ref.1, s32[2,128]{1,0:T(2,128)} %t_ref.1, f32[2,128]{1,0:T(2,128)} %g_ref.1), custom_call_target="tpu_custom_call" | custom-call | flops 1600000000 | bytes 5242880 | tf_op jit(solution)/shard_map/output_layer/pallas_call | solution.py:492
  61.8 2.5 %settle.1 = (bf16[16,256]{1,0:T(8,128)(2,1)}, bf16[4096,256]{1,0:T(8,128)(2,1)}, f32[2,128]{1,0:T(2,128)}) custom-call(bf16[16,256]{1,0:T(8,128)(2,1)} %get-tuple-element.9.dh, bf16[4096,256]{1,0:T(8,128)(2,1)} %get-tuple-element.10.dw, f32[2,128]{1,0:T(2,128)} %get-tuple-element.11.loss), custom_call_target="tpu_custom_call" | custom-call | tf_op jit(solution)/shard_map/settle/pallas_call | solution.py:533

commit v5 on v4

--- a/solution.py
+++ b/solution.py
@@ -327,9 +327,10 @@
             to_core(u, chunk(u, o, 1))
 
     def weigh(u):
-        landed(e_all.at[1 - c, u], s["ac_r"].at[u])
-        for half in range(2):
-            rows = slice(half * HALF + u * SUB, half * HALF + (u + 1) * SUB)
+        for n, half in enumerate((c, 1 - c)):
+            if n == 1:
+                landed(e_all.at[1 - c, u], s["ac_r"].at[u])
+            rows = pl.ds(pl.multiple_of(half * HALF + u * SUB, SUB), SUB)
             e = e_all[half, u].reshape(NB * ROWS, SUB)
             v["acc"][half * 2 + u] = jnp.dot(e, wm[rows, :], preferred_element_type=F32)
 

time: 64.5 us -> 65.2 us (1.011)
  no operation moved by 1% of the time
where the time goes in v5:
time: 65.2 us; the launch traced here: 64.4 us
  Pallas kernels  63.7 us (98%)
    pallas_call x1, Pallas kernels, call(): pl.pallas_call(kernel, out_shape=(jax.ShapeDtypeStruct((ROWS, CHUNK), BF1...  61.3 us
    pallas_call x1, Pallas kernels, on_device(): pl.pallas_call(settle, out_shape=[jax.ShapeDtypeStruct(x.shape, x.dtype)...  2.45 us

profile of v5, /device:TPU:1, one launch (start us, length us, event | category | flops | bytes accessed | tf_op | source)
XLA Modules:
  0.0 64.4 jit_solution(12933595789174427361)
XLA Ops:
  0.6 61.3 %output_layer.1 = (bf16[16,256]{1,0:T(8,128)(2,1)}, bf16[4096,256]{1,0:T(8,128)(2,1)}, f32[2,128]{1,0:T(2,128)}) custom-call(bf16[16,256]{1,0:T(8,128)(2,1)} %bitcast.3, bf16[4096,256]{1,0:T(8,128)(2,1)} %w_ref.1, s32[2,128]{1,0:T(2,128)} %t_ref.1, f32[2,128]{1,0:T(2,128)} %g_ref.1), custom_call_target="tpu_custom_call" | custom-call | flops 1600000000 | bytes 5242880 | tf_op jit(solution)/shard_map/output_layer/pallas_call | solution.py:493
  61.9 2.5 %settle.1 = (bf16[16,256]{1,0:T(8,128)(2,1)}, bf16[4096,256]{1,0:T(8,128)(2,1)}, f32[2,128]{1,0:T(2,128)}) custom-call(bf16[16,256]{1,0:T(8,128)(2,1)} %get-tuple-element.9.dh, bf16[4096,256]{1,0:T(8,128)(2,1)} %get-tuple-element.10.dw, f32[2,128]{1,0:T(2,128)} %get-tuple-element.11.loss), custom_call_target="tpu_custom_call" | custom-call | tf_op jit(solution)/shard_map/settle/pallas_call | solution.py:534
